TPU v7x, 32 devices: a whole 2x2x4 slice. The times are simulated.
32 devices in a mesh: batch: 4 (over x, core), ctx: 8 (over z, y).
Axes of the slice: x: 2, y: 2, z: 4, core: 2. Of those that a mesh axis runs over, the one named last changes fastest.
Arguments:
- lengths: int32 [64], P('batch'), parts along dimension 0, may hold values from 1 to 2560, 4096 in all
- queries: bfloat16 [16384, 512], P(('batch', 'ctx')), parts along dimension 0, may hold values from -256 to 256
- key_rows: bfloat16 [16384, 128], P(('batch', 'ctx')), parts along dimension 0, may hold values from -4.5 to 4.5
- values: bfloat16 [16384, 128], P(('batch', 'ctx')), parts along dimension 0, may hold values from -6 to 6
Outputs:
- attended: bfloat16 [16384, 512], P(('batch', 'ctx')), parts along dimension 0
- log_mass: float32 [4, 16384], P(None, ('batch', 'ctx')), parts along dimension 1
There are 4 independent parts, one for each index of `batch`. A program takes and returns all parts, laid end to end along the dimension named above; each array names one. Nothing has to cross between parts.
Inputs may be any that keep to these rules, and one draw needn't show every extreme that they name: The lengths sum to 4096; the longest is exactly 2560.
All inputs are finite; a program needn't handle non-finite values.
Results may differ from a plain program's by a relative error of at most 0.0035.
Values may be sent and summed in bfloat16 or wider, within the bound.
No kernel may reach another device: no remote copies, remote signals or barrier semaphores. Data moves between devices by JAX's collectives and lax.ppermute only.
A program may use at most 64 MiB of HBM per device.

v0:
```python
import functools
import math

import jax
import jax.numpy as jnp
from jax import lax
from jax.experimental import pallas as pl
from jax.experimental.pallas import tpu as pltpu
from jax.sharding import PartitionSpec as P

QH = 4
HD = 128
LOW = -1e30
SCALE = 1.0 / math.sqrt(HD)
EXP2_SCALE = SCALE * math.log2(math.e)
VMEM_LIMIT = 32 * 1024 * 1024
LITTLE = pl.CostEstimate(flops=1024, bytes_accessed=1024, transcendentals=0)


def dot(a, b):
    return jnp.dot(a, b, preferred_element_type=jnp.float32)


def own_kernel(lengths_ref, q_ref, kv_ref, qt_ref, acc_ref, stat_ref):
    q_rows = q_ref.shape[0]
    tile = math.gcd(q_rows, 128)
    own_first = lax.axis_index("ctx") * q_rows
    ends = []
    end = jnp.int32(0)
    for d in range(lengths_ref.shape[0]):
        end = end + lengths_ref[d]
        ends.append(end - own_first)
    values_t = jnp.transpose(kv_ref[1])
    for h in range(QH):
        qt_ref[h] = jnp.transpose(q_ref[:, h * HD : (h + 1) * HD])
    for t in range(q_rows // tile):
        keys = (t + 1) * tile
        here = slice(t * tile, (t + 1) * tile)
        row = lax.broadcasted_iota(jnp.int32, (1, tile), 1) + t * tile
        start = jnp.zeros((1, tile), jnp.int32)
        for end in ends:
            start = jnp.where(row >= end, jnp.maximum(start, end), start)
        key = lax.broadcasted_iota(jnp.int32, (keys, tile), 0)
        hidden = (key < start) | (key > row)
        hidden = jnp.concatenate([hidden] * QH, axis=1)
        heads = jnp.concatenate([qt_ref[h, :, here] for h in range(QH)], axis=1)
        scores = jnp.where(hidden, LOW, dot(kv_ref[0, :keys, :], heads))
        top = jnp.max(scores, axis=0, keepdims=True)
        weights = jnp.exp2((scores - top) * EXP2_SCALE)
        total = jnp.sum(weights, axis=0, keepdims=True)
        mixed = dot(values_t[:, :keys], weights.astype(jnp.bfloat16))
        for h in range(QH):
            part = slice(h * tile, (h + 1) * tile)
            acc_ref[h, :, here] = mixed[:, part]
            stat_ref[h : h + 1, here] = top[:, part]
            stat_ref[QH + h : QH + h + 1, here] = total[:, part]


def past_kernel(distances, is_last, lengths_ref, qt_ref, acc_in, stat_in, *refs):
    kv_refs = refs[: len(distances)]
    acc_ref, stat_ref = refs[len(distances) : len(distances) + 2]
    q_rows = qt_ref.shape[2]
    tile = math.gcd(q_rows, 256)
    half = q_rows // 2
    here = lax.axis_index("ctx")
    odd = here % 2
    own_first = here * q_rows
    first = own_first
    last = own_first
    end = jnp.int32(0)
    for d in range(lengths_ref.shape[0]):
        begin, end = end, end + lengths_ref[d]
        holds = (begin < own_first) & (end > own_first)
        first = jnp.where(holds, begin, first)
        last = jnp.where(holds, end, last)
    live_rows = last - own_first

    def side_by_side(read):
        return jnp.concatenate([read(h) for h in range(QH)], axis=1)

    def absorb(kv_ref, t, skipped=0, cut=None):
        cols = slice(t * tile, (t + 1) * tile)
        live = lax.broadcasted_iota(jnp.int32, (1, tile), 1) + t * tile < live_rows
        live = side_by_side(lambda h: live)
        scores = dot(kv_ref[0, skipped:], side_by_side(lambda h: qt_ref[h, :, cols]))
        if cut is not None:
            hidden = lax.broadcasted_iota(jnp.int32, scores.shape, 0) + skipped < cut
            scores = jnp.where(hidden, LOW, scores)
        old_top = side_by_side(lambda h: stat_ref[h : h + 1, cols])
        old_total = side_by_side(lambda h: stat_ref[QH + h : QH + h + 1, cols])
        top = jnp.maximum(old_top, jnp.max(scores, axis=0, keepdims=True))
        top = jnp.where(live, top, old_top)
        weights = jnp.exp2((scores - top) * EXP2_SCALE)
        total = jnp.sum(weights, axis=0, keepdims=True)
        mixed = dot(jnp.transpose(kv_ref[1, skipped:]), weights.astype(jnp.bfloat16))
        decay = jnp.exp2((old_top - top) * EXP2_SCALE)
        total = old_total * decay + jnp.where(live, total, 0.0)
        mixed = jnp.where(live, mixed, 0.0)
        for h in range(QH):
            part = slice(h * tile, (h + 1) * tile)
            acc_ref[h, :, cols] = acc_ref[h, :, cols] * decay[:, part] + mixed[:, part]
            stat_ref[h : h + 1, cols] = top[:, part]
            stat_ref[QH + h : QH + h + 1, cols] = total[:, part]

    for kv_ref, (even_distance, odd_distance) in zip(kv_refs, distances):
        distance = jnp.where(odd == 1, odd_distance, even_distance)
        cut = first - (here - distance) * q_rows
        for t in range(q_rows // tile):
            seen = (distance > 0) & (live_rows > t * tile) & (cut < q_rows)
            pl.when(seen & (cut <= 0))(functools.partial(absorb, kv_ref, t))
            pl.when(seen & (cut > 0) & (cut < half))(
                functools.partial(absorb, kv_ref, t, 0, cut)
            )
            pl.when(seen & (cut >= half))(functools.partial(absorb, kv_ref, t, half, cut))

    if is_last:
        out_hbm, mass_ref, out_ref, sem = refs[len(distances) + 2 :]
        copies = []
        for t in range(q_rows // tile):
            rows_at = slice(t * tile, (t + 1) * tile)
            for h in range(QH):
                share = 1.0 / stat_ref[QH + h : QH + h + 1, rows_at]
                mixed = (acc_ref[h, :, rows_at] * share).astype(jnp.bfloat16)
                out_ref[rows_at, h * HD : (h + 1) * HD] = jnp.transpose(mixed)
            copy = pltpu.make_async_copy(
                out_ref.at[pl.ds(t * tile, tile), :],
                out_hbm.at[pl.ds(t * tile, tile), :],
                sem.at[t],
            )
            copy.start()
            copies.append(copy)
        mass_ref[...] = stat_ref[:QH, :] * SCALE + jnp.log(stat_ref[QH:, :])
        for copy in copies:
            copy.wait()


def state_shapes(q_rows):
    return (
        jax.ShapeDtypeStruct((QH, HD, q_rows), jnp.float32),
        jax.ShapeDtypeStruct((2 * QH, q_rows), jnp.float32),
    )


def own_part(lengths, queries, own):
    q_rows = queries.shape[0]
    in_smem = pl.BlockSpec(memory_space=pltpu.SMEM)
    in_vmem = pl.BlockSpec(memory_space=pltpu.VMEM)
    qt, *state = pl.pallas_call(
        own_kernel,
        out_shape=(jax.ShapeDtypeStruct((QH, HD, q_rows), jnp.bfloat16),) + state_shapes(q_rows),
        in_specs=[in_smem, in_vmem, in_vmem],
        out_specs=(in_vmem, in_vmem, in_vmem),
        compiler_params=pltpu.CompilerParams(vmem_limit_bytes=VMEM_LIMIT),
        cost_estimate=LITTLE,
    )(lengths, queries, own)
    return qt, state


def past_part(lengths, qt, state, shards, is_last=False):
    q_rows = qt.shape[2]
    distances = [s[0] for s in shards]
    arrays = [s[1] for s in shards]
    in_smem = pl.BlockSpec(memory_space=pltpu.SMEM)
    in_vmem = pl.BlockSpec(memory_space=pltpu.VMEM)
    out_shape = state_shapes(q_rows)
    out_specs = (in_vmem, in_vmem)
    scratch = []
    if is_last:
        out = jax.ShapeDtypeStruct((q_rows, QH * HD), jnp.bfloat16)
        out_shape += (out, jax.ShapeDtypeStruct((QH, q_rows), jnp.float32))
        out_specs += (pl.BlockSpec(memory_space=pl.ANY), in_vmem)
        tiles = q_rows // math.gcd(q_rows, 256)
        scratch = [pltpu.VMEM(out.shape, out.dtype), pltpu.SemaphoreType.DMA((tiles,))]
    outs = pl.pallas_call(
        functools.partial(past_kernel, distances, is_last),
        out_shape=out_shape,
        in_specs=[in_smem] + [in_vmem] * (3 + len(arrays)),
        out_specs=out_specs,
        scratch_shapes=scratch,
        input_output_aliases={2: 0, 3: 1},
        compiler_params=pltpu.CompilerParams(vmem_limit_bytes=VMEM_LIMIT),
        cost_estimate=LITTLE,
    )(lengths, qt, *state, *arrays)
    return outs[2:] if is_last else outs


def on_device(lengths, queries, key_rows, values):
    count = lax.axis_size("ctx")
    reach = min(count // 2 + 1, count - 1)
    strides = reach // 2

    def send(value, pairs):
        return lax.ppermute(value, "ctx", pairs)

    own = jnp.stack([key_rows, values])
    moving = send(own, [(i, i + 2) for i in range(count - 2)])
    qt, state = own_part(lengths, queries, own)
    own, *state = lax.optimization_barrier((own, *state))
    pairs = [(i, i + 1) for i in range(0, count, 2)]
    if reach % 2 == 1:
        pairs += [(i + 1, i) for i in range(0, count - reach - 1, 2)]
    beside = first_beside = send(own, pairs)
    moving, *state = lax.optimization_barrier((moving, *state))
    side = [((0, 1), beside)]
    for k in range(1, strides + 1):
        arrived = moving
        if k < strides:
            moving = send(arrived, [(i, i + 2) for i in range(2 * k, count - 2)])
        exchange = [(i + 1, i) for i in range(2 * k, count, 2)]
        distances = (2 * k - 1, 0)
        if 2 * k + 1 <= reach:
            exchange += [(i, i + 1) for i in range(2 * k, count, 2)]
            distances = (2 * k - 1, 2 * k + 1)
        shards = [((2 * k, 2 * k), arrived)] + (side if k > 1 else [])
        side = (side if k == 1 else []) + [(distances, send(arrived, exchange))]
        state = past_part(lengths, qt, state, shards)
        if k == strides - 1 and reach % 2 == 1:
            first_beside, *state = lax.optimization_barrier((first_beside, *state))
            far = send(first_beside, [(i, i + reach + 1) for i in range(0, count - reach - 1, 2)])
        if k < strides:
            moving, *state = lax.optimization_barrier((moving, *state))
    if reach % 2 == 1:
        side.insert(0, ((reach, 0), far))
    return past_part(lengths, qt, state, side, is_last=True)


def solution(mesh):
    in_specs = (
        P("batch"),
        P(("batch", "ctx"), None),
        P(("batch", "ctx"), None),
        P(("batch", "ctx"), None),
    )
    out_specs = (P(("batch", "ctx"), None), P(None, ("batch", "ctx")))
    return jax.shard_map(
        on_device, mesh=mesh, in_specs=in_specs, out_specs=out_specs, check_vma=False
    )
```

profile of v0, /device:TPU:16, one launch (start us, length us, event | category | flops | bytes accessed | tf_op | source)
XLA Modules:
  0.0 35.0 jit_solution(15504877423422346831)
XLA Ops:
  0.6 0.0 copy-start
  0.6 0.0 copy-start.1
  0.7 1.0 %pad_maximum_fusion.kv_ref = bf16[2,512,128]{2,1,0:T(8,128)(2,1)S(1)} fusion(bf16[1,512,128]{2,1,0:T(8,128)(2,1)} %bitcast.2, bf16[1,512,128]{2,1,0:T(8,128)(2,1)} %bitcast.3), kind=kLoop, calls=%fused_computation | loop fusion | flops 131072 | bytes 524288 | tf_op jit(solution)/shard_map/stack | solution.py:195
  1.7 3.5 %collective-permute-start = (bf16[2,512,128]{2,1,0:T(8,128)(2,1)S(1)}, bf16[2,512,128]{2,1,0:T(8,128)(2,1)S(1)}, u32[]{:S(2)}, u32[]{:S(2)}) collective-permute-start(bf16[2,512,128]{2,1,0:T(8,128)(2,1)S(1)} %pad_maximum_fusion.kv_ref), channel_id=1, source_target_pairs={{0,2},{1,3},{2,4},{3,5},{4,6},{5,7},{8,10},{9,11},{10,12},{11,13},... | collective-permute-start | bytes 786440 | tf_op jit(solution)/shard_map/ppermute | solution.py:193
  5.2 0.0 copy-done
  5.2 0.0 copy-done.1
  5.2 2.3 %shard_map.59 = (bf16[4,128,512]{2,1,0:T(8,128)(2,1)S(1)}, f32[4,128,512]{2,1,0:T(8,128)S(1)}, f32[8,512]{1,0:T(8,128)S(1)}) custom-call(s32[16]{0:T(128)S(1)} %copy-done.1, bf16[512,512]{1,0:T(8,128)(2,1)S(1)} %copy-done, bf16[2,512,128]{2,1,0:T(8,128)(2,1)S(1)} %pad_maximum_fusion.kv_ref), custom_call_target="tpu_custom_call" | custom-call | flops 1024 | bytes 1024 | tf_op jit(solution)/shard_map/pallas_call | solution.py:148
  7.6 3.4 %collective-permute-start.2 = (bf16[2,512,128]{2,1,0:T(8,128)(2,1)S(1)}, bf16[2,512,128]{2,1,0:T(8,128)(2,1)S(1)}, u32[]{:S(2)}, u32[]{:S(2)}) collective-permute-start(bf16[2,512,128]{2,1,0:T(8,128)(2,1)S(1)} %pad_maximum_fusion.kv_ref), channel_id=1, source_target_pairs={{0,1},{2,3},{4,5},{6,7},{1,0},{8,9},{10,11},{12,13},{14,15},{9,8},... | collective-permute-start | bytes 786440 | tf_op jit(solution)/shard_map/ppermute | solution.py:193
  11.0 0.6 %collective-permute-done.refs_0_ = bf16[2,512,128]{2,1,0:T(8,128)(2,1)S(1)} collective-permute-done((bf16[2,512,128]{2,1,0:T(8,128)(2,1)S(1)}, bf16[2,512,128]{2,1,0:T(8,128)(2,1)S(1)}, u32[]{:S(2)}, u32[]{:S(2)}) %collective-permute-start) | collective-permute-done | bytes 262176 | tf_op jit(solution)/shard_map/ppermute | solution.py:193
  11.6 3.5 %collective-permute-start.1 = (bf16[2,512,128]{2,1,0:T(8,128)(2,1)S(1)}, bf16[2,512,128]{2,1,0:T(8,128)(2,1)S(1)}, u32[]{:S(2)}, u32[]{:S(2)}) collective-permute-start(bf16[2,512,128]{2,1,0:T(8,128)(2,1)S(1)} %collective-permute-done.refs_0_), channel_id=1, source_target_pairs={{2,4},{3,5},{4,6},{5,7},{10,12},{11,13},{12,14},{13,15},{18,20},{1... | collective-permute-start | bytes 786440 | tf_op jit(solution)/shard_map/ppermute | solution.py:193
  15.1 3.4 %collective-permute-start.3 = (bf16[2,512,128]{2,1,0:T(8,128)(2,1)S(1)}, bf16[2,512,128]{2,1,0:T(8,128)(2,1)S(1)}, u32[]{:S(2)}, u32[]{:S(2)}) collective-permute-start(bf16[2,512,128]{2,1,0:T(8,128)(2,1)S(1)} %collective-permute-done.refs_0_), channel_id=1, source_target_pairs={{3,2},{5,4},{7,6},{2,3},{4,5},{6,7},{11,10},{13,12},{15,14},{10,11... | collective-permute-start | bytes 786440 | tf_op jit(solution)/shard_map/ppermute | solution.py:193
  18.6 2.6 %shard_map.60 = (f32[4,128,512]{2,1,0:T(8,128)S(1)}, f32[8,512]{1,0:T(8,128)S(1)}) custom-call(s32[16]{0:T(128)S(1)} %copy-done.1, bf16[4,128,512]{2,1,0:T(8,128)(2,1)S(1)} %get-tuple-element.23.qt_ref, f32[4,128,512]{2,1,0:T(8,128)S(1)} %get-tuple-element.30.acc_in, ...), custom_call_target="tpu_custom_call", output_to_operand_aliasing={{0}: (2, {}), {1}: (3, {})} | custom-call | flops 1024 | bytes 1024 | tf_op jit(solution)/shard_map/pallas_call | solution.py:174
  21.2 0.0 collective-permute-done.2.refs_1_
  21.2 0.7 %collective-permute-start.4 = (bf16[2,512,128]{2,1,0:T(8,128)(2,1)S(1)}, bf16[2,512,128]{2,1,0:T(8,128)(2,1)S(1)}, u32[]{:S(2)}, u32[]{:S(2)}) collective-permute-start(bf16[2,512,128]{2,1,0:T(8,128)(2,1)S(1)} %collective-permute-done.2.refs_1_), channel_id=1, source_target_pairs={{0,6},{8,14},{16,22},{24,30}} | collective-permute-start | bytes 786440 | tf_op jit(solution)/shard_map/ppermute | solution.py:193
  21.9 0.0 collective-permute-done.1.refs_0_
  21.9 2.2 %collective-permute-start.5 = (bf16[2,512,128]{2,1,0:T(8,128)(2,1)S(1)}, bf16[2,512,128]{2,1,0:T(8,128)(2,1)S(1)}, u32[]{:S(2)}, u32[]{:S(2)}) collective-permute-start(bf16[2,512,128]{2,1,0:T(8,128)(2,1)S(1)} %collective-permute-done.1.refs_0_), channel_id=1, source_target_pairs={{5,4},{7,6},{4,5},{6,7},{13,12},{15,14},{12,13},{14,15},{21,20},{2... | collective-permute-start | bytes 786440 | tf_op jit(solution)/shard_map/ppermute | solution.py:193
  24.1 0.0 collective-permute-done.3.refs_2_
  24.1 5.0 %shard_map.61 = (f32[4,128,512]{2,1,0:T(8,128)S(1)}, f32[8,512]{1,0:T(8,128)S(1)}) custom-call(s32[16]{0:T(128)S(1)} %copy-done.1, bf16[4,128,512]{2,1,0:T(8,128)(2,1)S(1)} %get-tuple-element.23.qt_ref, f32[4,128,512]{2,1,0:T(8,128)S(1)} %get-tuple-element.36.acc_in, ...), custom_call_target="tpu_custom_call", output_to_operand_aliasing={{0}: (2, {}), {1}: (3, {})} | custom-call | flops 1024 | bytes 1024 | tf_op jit(solution)/shard_map/pallas_call | solution.py:174
  29.2 0.0 collective-permute-done.4.refs_0_
  29.2 1.2 %collective-permute-done.5.refs_1_ = bf16[2,512,128]{2,1,0:T(8,128)(2,1)S(1)} collective-permute-done((bf16[2,512,128]{2,1,0:T(8,128)(2,1)S(1)}, bf16[2,512,128]{2,1,0:T(8,128)(2,1)S(1)}, u32[]{:S(2)}, u32[]{:S(2)}) %collective-permute-start.5) | collective-permute-done | bytes 262176 | tf_op jit(solution)/shard_map/ppermute | solution.py:193
  30.4 4.4 %shard_map.62 = (f32[4,128,512]{2,1,0:T(8,128)S(1)}, f32[8,512]{1,0:T(8,128)S(1)}, bf16[512,512]{1,0:T(8,128)(2,1)}, f32[4,512]{1,0:T(4,128)}) custom-call(s32[16]{0:T(128)S(1)} %copy-done.1, bf16[4,128,512]{2,1,0:T(8,128)(2,1)S(1)} %get-tuple-element.23.qt_ref, ...), custom_call_target="tpu_custom_call", output_to_operand_aliasing={{0}: (2, {}), {1}: (3, {})} | custom-call | flops 1024 | bytes 1024 | tf_op jit(solution)/shard_map/pallas_call | solution.py:174
Async XLA Ops:
  0.6 4.6 %copy-start = (bf16[512,512]{1,0:T(8,128)(2,1)S(1)}, bf16[512,512]{1,0:T(8,128)(2,1)}, u32[]{:S(2)}) copy-start(bf16[512,512]{1,0:T(8,128)(2,1)} %q_ref.1) | copy-start | bytes 1572868
  0.6 4.6 %copy-start.1 = (s32[16]{0:T(128)S(1)}, s32[16]{0:T(128)}, u32[]{:S(2)}) copy-start(s32[16]{0:T(128)} %lengths_ref.7) | copy-start | bytes 196
  1.7 9.9 %collective-permute-start = (bf16[2,512,128]{2,1,0:T(8,128)(2,1)S(1)}, bf16[2,512,128]{2,1,0:T(8,128)(2,1)S(1)}, u32[]{:S(2)}, u32[]{:S(2)}) collective-permute-start(bf16[2,512,128]{2,1,0:T(8,128)(2,1)S(1)} %pad_maximum_fusion.kv_ref), channel_id=1, source_target_pairs={{0,2},{1,3},{2,4},{3,5},{4,6},{5,7},{8,10},{9,11},{10,12},{11,13},... | collective-permute-start | bytes 786440 | tf_op jit(solution)/shard_map/ppermute | solution.py:193
  7.6 13.6 %collective-permute-start.2 = (bf16[2,512,128]{2,1,0:T(8,128)(2,1)S(1)}, bf16[2,512,128]{2,1,0:T(8,128)(2,1)S(1)}, u32[]{:S(2)}, u32[]{:S(2)}) collective-permute-start(bf16[2,512,128]{2,1,0:T(8,128)(2,1)S(1)} %pad_maximum_fusion.kv_ref), channel_id=1, source_target_pairs={{0,1},{2,3},{4,5},{6,7},{1,0},{8,9},{10,11},{12,13},{14,15},{9,8},... | collective-permute-start | bytes 786440 | tf_op jit(solution)/shard_map/ppermute | solution.py:193
  11.6 10.3 %collective-permute-start.1 = (bf16[2,512,128]{2,1,0:T(8,128)(2,1)S(1)}, bf16[2,512,128]{2,1,0:T(8,128)(2,1)S(1)}, u32[]{:S(2)}, u32[]{:S(2)}) collective-permute-start(bf16[2,512,128]{2,1,0:T(8,128)(2,1)S(1)} %collective-permute-done.refs_0_), channel_id=1, source_target_pairs={{2,4},{3,5},{4,6},{5,7},{10,12},{11,13},{12,14},{13,15},{18,20},{1... | collective-permute-start | bytes 786440 | tf_op jit(solution)/shard_map/ppermute | solution.py:193
  15.1 9.0 %collective-permute-start.3 = (bf16[2,512,128]{2,1,0:T(8,128)(2,1)S(1)}, bf16[2,512,128]{2,1,0:T(8,128)(2,1)S(1)}, u32[]{:S(2)}, u32[]{:S(2)}) collective-permute-start(bf16[2,512,128]{2,1,0:T(8,128)(2,1)S(1)} %collective-permute-done.refs_0_), channel_id=1, source_target_pairs={{3,2},{5,4},{7,6},{2,3},{4,5},{6,7},{11,10},{13,12},{15,14},{10,11... | collective-permute-start | bytes 786440 | tf_op jit(solution)/shard_map/ppermute | solution.py:193
  21.2 8.0 %collective-permute-start.4 = (bf16[2,512,128]{2,1,0:T(8,128)(2,1)S(1)}, bf16[2,512,128]{2,1,0:T(8,128)(2,1)S(1)}, u32[]{:S(2)}, u32[]{:S(2)}) collective-permute-start(bf16[2,512,128]{2,1,0:T(8,128)(2,1)S(1)} %collective-permute-done.2.refs_1_), channel_id=1, source_target_pairs={{0,6},{8,14},{16,22},{24,30}} | collective-permute-start | bytes 786440 | tf_op jit(solution)/shard_map/ppermute | solution.py:193
  21.9 8.5 %collective-permute-start.5 = (bf16[2,512,128]{2,1,0:T(8,128)(2,1)S(1)}, bf16[2,512,128]{2,1,0:T(8,128)(2,1)S(1)}, u32[]{:S(2)}, u32[]{:S(2)}) collective-permute-start(bf16[2,512,128]{2,1,0:T(8,128)(2,1)S(1)} %collective-permute-done.1.refs_0_), channel_id=1, source_target_pairs={{5,4},{7,6},{4,5},{6,7},{13,12},{15,14},{12,13},{14,15},{21,20},{2... | collective-permute-start | bytes 786440 | tf_op jit(solution)/shard_map/ppermute | solution.py:193
where the time goes:
time: 35.5 us; the launch traced here: 35 us
  starting transfers between devices  16.7 us (47%)
  Pallas kernels  14.4 us (41%)
  waiting for transfers between devices  1.86 us (5%)
  other arithmetic  1.05 us (3%)
  between operations  0.95 us (3%)
    ppermute x6, starting transfers between devices, send(): return lax.ppermute(value, 'ctx', pairs)  16.7 us
    pallas_call x3, Pallas kernels, past_part(): pl.pallas_call(functools.partial(past_kernel, distances, is_last), out_sh...  12.1 us
    pallas_call x1, Pallas kernels, own_part(): pl.pallas_call(own_kernel, out_shape=(jax.ShapeDtypeStruct((QH, HD, q_row...  2.34 us
    ppermute x6, waiting for transfers between devices, send(): return lax.ppermute(value, 'ctx', pairs)  1.86 us
    another operation x1, other arithmetic, on_device(): own = jnp.stack([key_rows, values])  1.05 us
  transfers between devices with their start and end apart: 6, of which 2 were waited for; matrix products, arithmetic and copies ran while one was open for 0% of the time, Pallas kernels for 29%

commit v1 on v0

--- a/solution.py
+++ b/solution.py
@@ -114,24 +114,11 @@
             pl.when(seen & (cut >= half))(functools.partial(absorb, kv_ref, t, half, cut))
 
     if is_last:
-        out_hbm, mass_ref, out_ref, sem = refs[len(distances) + 2 :]
-        copies = []
-        for t in range(q_rows // tile):
-            rows_at = slice(t * tile, (t + 1) * tile)
-            for h in range(QH):
-                share = 1.0 / stat_ref[QH + h : QH + h + 1, rows_at]
-                mixed = (acc_ref[h, :, rows_at] * share).astype(jnp.bfloat16)
-                out_ref[rows_at, h * HD : (h + 1) * HD] = jnp.transpose(mixed)
-            copy = pltpu.make_async_copy(
-                out_ref.at[pl.ds(t * tile, tile), :],
-                out_hbm.at[pl.ds(t * tile, tile), :],
-                sem.at[t],
-            )
-            copy.start()
-            copies.append(copy)
+        out_ref, mass_ref = refs[len(distances) + 2 :]
+        for h in range(QH):
+            mixed = acc_ref[h] * (1.0 / stat_ref[QH + h : QH + h + 1, :])
+            out_ref[:, h * HD : (h + 1) * HD] = jnp.transpose(mixed.astype(jnp.bfloat16))
         mass_ref[...] = stat_ref[:QH, :] * SCALE + jnp.log(stat_ref[QH:, :])
-        for copy in copies:
-            copy.wait()
 
 
 def state_shapes(q_rows):
@@ -163,20 +150,16 @@
     in_smem = pl.BlockSpec(memory_space=pltpu.SMEM)
     in_vmem = pl.BlockSpec(memory_space=pltpu.VMEM)
     out_shape = state_shapes(q_rows)
-    out_specs = (in_vmem, in_vmem)
-    scratch = []
     if is_last:
-        out = jax.ShapeDtypeStruct((q_rows, QH * HD), jnp.bfloat16)
-        out_shape += (out, jax.ShapeDtypeStruct((QH, q_rows), jnp.float32))
-        out_specs += (pl.BlockSpec(memory_space=pl.ANY), in_vmem)
-        tiles = q_rows // math.gcd(q_rows, 256)
-        scratch = [pltpu.VMEM(out.shape, out.dtype), pltpu.SemaphoreType.DMA((tiles,))]
+        out_shape += (
+            jax.ShapeDtypeStruct((q_rows, QH * HD), jnp.bfloat16),
+            jax.ShapeDtypeStruct((QH, q_rows), jnp.float32),
+        )
     outs = pl.pallas_call(
         functools.partial(past_kernel, distances, is_last),
         out_shape=out_shape,
         in_specs=[in_smem] + [in_vmem] * (3 + len(arrays)),
-        out_specs=out_specs,
-        scratch_shapes=scratch,
+        out_specs=(in_vmem,) * len(out_shape),
         input_output_aliases={2: 0, 3: 1},
         compiler_params=pltpu.CompilerParams(vmem_limit_bytes=VMEM_LIMIT),
         cost_estimate=LITTLE,
@@ -196,32 +179,31 @@
     moving = send(own, [(i, i + 2) for i in range(count - 2)])
     qt, state = own_part(lengths, queries, own)
     own, *state = lax.optimization_barrier((own, *state))
-    pairs = [(i, i + 1) for i in range(0, count, 2)]
+    beside = send(own, [(i, i + 1) for i in range(0, count, 2)])
+    side = [((0, 1), beside)]
     if reach % 2 == 1:
-        pairs += [(i + 1, i) for i in range(0, count - reach - 1, 2)]
-    beside = first_beside = send(own, pairs)
+        far = send(own, [(i, i + reach) for i in range(1, count - reach, 2)])
+        side.append(((reach, 0), far))
     moving, *state = lax.optimization_barrier((moving, *state))
-    side = [((0, 1), beside)]
     for k in range(1, strides + 1):
         arrived = moving
+        shards = [((2 * k, 2 * k), arrived)] + side
         if k < strides:
             moving = send(arrived, [(i, i + 2) for i in range(2 * k, count - 2)])
-        exchange = [(i + 1, i) for i in range(2 * k, count, 2)]
-        distances = (2 * k - 1, 0)
-        if 2 * k + 1 <= reach:
+            exchange = [(i + 1, i) for i in range(2 * k, count, 2)]
             exchange += [(i, i + 1) for i in range(2 * k, count, 2)]
-            distances = (2 * k - 1, 2 * k + 1)
-        shards = [((2 * k, 2 * k), arrived)] + (side if k > 1 else [])
-        side = (side if k == 1 else []) + [(distances, send(arrived, exchange))]
+            side = [((2 * k - 1, 2 * k + 1), send(arrived, exchange))]
+        if k == strides - 1:
+            across = [(i, i + 1) for i in range(2 * k + 1, count - 1, 2)]
+            across_distances = (2 * k + 1, 0)
+            if 2 * k + 3 <= reach:
+                across += [(i, i + 3) for i in range(2 * k, count - 3, 2)]
+                across_distances = (2 * k + 1, 2 * k + 3)
+            late = [(across_distances, send(arrived, across))]
         state = past_part(lengths, qt, state, shards)
-        if k == strides - 1 and reach % 2 == 1:
-            first_beside, *state = lax.optimization_barrier((first_beside, *state))
-            far = send(first_beside, [(i, i + reach + 1) for i in range(0, count - reach - 1, 2)])
         if k < strides:
             moving, *state = lax.optimization_barrier((moving, *state))
-    if reach % 2 == 1:
-        side.insert(0, ((reach, 0), far))
-    return past_part(lengths, qt, state, side, is_last=True)
+    return past_part(lengths, qt, state, late, is_last=True)
 
 
 def solution(mesh):

time: 35.5 us -> 40.4 us (1.14)
  the two profiles are of different devices: /device:TPU:16 before, /device:TPU:24 now
where the time goes in v1:
time: 40.4 us; the launch traced here: 41.1 us
  Pallas kernels  15.1 us (37%)
  waiting for transfers between devices  12.2 us (30%)
  starting transfers between devices  12 us (30%)
  other arithmetic  1.05 us (3%)
  between operations  0.76 us (2%)
    pallas_call x3, Pallas kernels, past_part(): pl.pallas_call(functools.partial(past_kernel, distances, is_last), out_sh...  12.7 us
    ppermute x6, waiting for transfers between devices, send(): return lax.ppermute(value, 'ctx', pairs)  12.2 us
    ppermute x6, starting transfers between devices, send(): return lax.ppermute(value, 'ctx', pairs)  12 us
    pallas_call x1, Pallas kernels, own_part(): pl.pallas_call(own_kernel, out_shape=(jax.ShapeDtypeStruct((QH, HD, q_row...  2.34 us
    another operation x1, other arithmetic, on_device(): own = jnp.stack([key_rows, values])  1.05 us
  transfers between devices with their start and end apart: 6, of which 3 were waited for; matrix products, arithmetic and copies ran while one was open for 0% of the time, Pallas kernels for 28%

profile of v1, /device:TPU:24, one launch (start us, length us, event | category | flops | bytes accessed | tf_op | source)
XLA Modules:
  0.0 41.1 jit_solution(4203685813964977184)
XLA Ops:
  0.6 0.0 copy-start
  0.6 0.0 copy-start.1
  0.7 1.0 %pad_maximum_fusion.kv_ref = bf16[2,512,128]{2,1,0:T(8,128)(2,1)S(1)} fusion(bf16[1,512,128]{2,1,0:T(8,128)(2,1)} %bitcast.2, bf16[1,512,128]{2,1,0:T(8,128)(2,1)} %bitcast.3), kind=kLoop, calls=%fused_computation | loop fusion | flops 131072 | bytes 524288 | tf_op jit(solution)/shard_map/stack | solution.py:178
  1.7 1.3 %collective-permute-start = (bf16[2,512,128]{2,1,0:T(8,128)(2,1)S(1)}, bf16[2,512,128]{2,1,0:T(8,128)(2,1)S(1)}, u32[]{:S(2)}, u32[]{:S(2)}) collective-permute-start(bf16[2,512,128]{2,1,0:T(8,128)(2,1)S(1)} %pad_maximum_fusion.kv_ref), channel_id=1, source_target_pairs={{0,2},{1,3},{2,4},{3,5},{4,6},{5,7},{8,10},{9,11},{10,12},{11,13},... | collective-permute-start | bytes 786440 | tf_op jit(solution)/shard_map/ppermute | solution.py:176
  3.0 0.0 copy-done
  3.0 0.0 copy-done.1
  3.0 2.3 %shard_map.59 = (bf16[4,128,512]{2,1,0:T(8,128)(2,1)S(1)}, f32[4,128,512]{2,1,0:T(8,128)S(1)}, f32[8,512]{1,0:T(8,128)S(1)}) custom-call(s32[16]{0:T(128)S(1)} %copy-done.1, bf16[512,512]{1,0:T(8,128)(2,1)S(1)} %copy-done, bf16[2,512,128]{2,1,0:T(8,128)(2,1)S(1)} %pad_maximum_fusion.kv_ref), custom_call_target="tpu_custom_call" | custom-call | flops 1024 | bytes 1024 | tf_op jit(solution)/shard_map/pallas_call | solution.py:135
  5.4 3.4 %collective-permute-start.2 = (bf16[2,512,128]{2,1,0:T(8,128)(2,1)S(1)}, bf16[2,512,128]{2,1,0:T(8,128)(2,1)S(1)}, u32[]{:S(2)}, u32[]{:S(2)}) collective-permute-start(bf16[2,512,128]{2,1,0:T(8,128)(2,1)S(1)} %pad_maximum_fusion.kv_ref), channel_id=1, source_target_pairs={{0,1},{2,3},{4,5},{6,7},{8,9},{10,11},{12,13},{14,15},{16,17},{18,... | collective-permute-start | bytes 786440 | tf_op jit(solution)/shard_map/ppermute | solution.py:176
  8.8 1.3 %collective-permute-start.3 = (bf16[2,512,128]{2,1,0:T(8,128)(2,1)S(1)}, bf16[2,512,128]{2,1,0:T(8,128)(2,1)S(1)}, u32[]{:S(2)}, u32[]{:S(2)}) collective-permute-start(bf16[2,512,128]{2,1,0:T(8,128)(2,1)S(1)} %pad_maximum_fusion.kv_ref), channel_id=1, source_target_pairs={{1,6},{9,14},{17,22},{25,30}} | collective-permute-start | bytes 786440 | tf_op jit(solution)/shard_map/ppermute | solution.py:176
  10.1 1.5 %collective-permute-done.refs_0_ = bf16[2,512,128]{2,1,0:T(8,128)(2,1)S(1)} collective-permute-done((bf16[2,512,128]{2,1,0:T(8,128)(2,1)S(1)}, bf16[2,512,128]{2,1,0:T(8,128)(2,1)S(1)}, u32[]{:S(2)}, u32[]{:S(2)}) %collective-permute-start) | collective-permute-done | bytes 262176 | tf_op jit(solution)/shard_map/ppermute | solution.py:176
  11.6 1.3 %collective-permute-start.1 = (bf16[2,512,128]{2,1,0:T(8,128)(2,1)S(1)}, bf16[2,512,128]{2,1,0:T(8,128)(2,1)S(1)}, u32[]{:S(2)}, u32[]{:S(2)}) collective-permute-start(bf16[2,512,128]{2,1,0:T(8,128)(2,1)S(1)} %collective-permute-done.refs_0_), channel_id=1, source_target_pairs={{2,4},{3,5},{4,6},{5,7},{10,12},{11,13},{12,14},{13,15},{18,20},{1... | collective-permute-start | bytes 786440 | tf_op jit(solution)/shard_map/ppermute | solution.py:176
  12.9 3.4 %collective-permute-start.4 = (bf16[2,512,128]{2,1,0:T(8,128)(2,1)S(1)}, bf16[2,512,128]{2,1,0:T(8,128)(2,1)S(1)}, u32[]{:S(2)}, u32[]{:S(2)}) collective-permute-start(bf16[2,512,128]{2,1,0:T(8,128)(2,1)S(1)} %collective-permute-done.refs_0_), channel_id=1, source_target_pairs={{3,2},{5,4},{7,6},{2,3},{4,5},{6,7},{11,10},{13,12},{15,14},{10,11... | collective-permute-start | bytes 786440 | tf_op jit(solution)/shard_map/ppermute | solution.py:176
  16.4 1.3 %collective-permute-start.5 = (bf16[2,512,128]{2,1,0:T(8,128)(2,1)S(1)}, bf16[2,512,128]{2,1,0:T(8,128)(2,1)S(1)}, u32[]{:S(2)}, u32[]{:S(2)}) collective-permute-start(bf16[2,512,128]{2,1,0:T(8,128)(2,1)S(1)} %collective-permute-done.refs_0_), channel_id=1, source_target_pairs={{3,4},{5,6},{2,5},{4,7},{11,12},{13,14},{10,13},{12,15},{19,20},{2... | collective-permute-start | bytes 786440 | tf_op jit(solution)/shard_map/ppermute | solution.py:176
  17.7 0.0 collective-permute-done.2.refs_1_
  17.7 3.7 %collective-permute-done.3.refs_2_ = bf16[2,512,128]{2,1,0:T(8,128)(2,1)S(1)} collective-permute-done((bf16[2,512,128]{2,1,0:T(8,128)(2,1)S(1)}, bf16[2,512,128]{2,1,0:T(8,128)(2,1)S(1)}, u32[]{:S(2)}, u32[]{:S(2)}) %collective-permute-start.3) | collective-permute-done | bytes 262176 | tf_op jit(solution)/shard_map/ppermute | solution.py:176
  21.4 4.2 %shard_map.60 = (f32[4,128,512]{2,1,0:T(8,128)S(1)}, f32[8,512]{1,0:T(8,128)S(1)}) custom-call(s32[16]{0:T(128)S(1)} %copy-done.1, bf16[4,128,512]{2,1,0:T(8,128)(2,1)S(1)} %get-tuple-element.20.qt_ref, f32[4,128,512]{2,1,0:T(8,128)S(1)} %get-tuple-element.26.acc_in, ...), custom_call_target="tpu_custom_call", output_to_operand_aliasing={{0}: (2, {}), {1}: (3, {})} | custom-call | flops 1024 | bytes 1024 | tf_op jit(solution)/shard_map/pallas_call | solution.py:158
  25.6 0.0 collective-permute-done.1.refs_0_
  25.6 6.9 %collective-permute-done.4.refs_1_ = bf16[2,512,128]{2,1,0:T(8,128)(2,1)S(1)} collective-permute-done((bf16[2,512,128]{2,1,0:T(8,128)(2,1)S(1)}, bf16[2,512,128]{2,1,0:T(8,128)(2,1)S(1)}, u32[]{:S(2)}, u32[]{:S(2)}) %collective-permute-start.4) | collective-permute-done | bytes 262176 | tf_op jit(solution)/shard_map/ppermute | solution.py:176
  32.5 4.9 %shard_map.61 = (f32[4,128,512]{2,1,0:T(8,128)S(1)}, f32[8,512]{1,0:T(8,128)S(1)}) custom-call(s32[16]{0:T(128)S(1)} %copy-done.1, bf16[4,128,512]{2,1,0:T(8,128)(2,1)S(1)} %get-tuple-element.20.qt_ref, f32[4,128,512]{2,1,0:T(8,128)S(1)} %get-tuple-element.31.acc_in, ...), custom_call_target="tpu_custom_call", output_to_operand_aliasing={{0}: (2, {}), {1}: (3, {})} | custom-call | flops 1024 | bytes 1024 | tf_op jit(solution)/shard_map/pallas_call | solution.py:158
  37.4 0.0 collective-permute-done.5.refs_0_
  37.5 3.6 %shard_map.62 = (f32[4,128,512]{2,1,0:T(8,128)S(1)}, f32[8,512]{1,0:T(8,128)S(1)}, bf16[512,512]{1,0:T(8,128)(2,1)}, f32[4,512]{1,0:T(4,128)}) custom-call(s32[16]{0:T(128)S(1)} %copy-done.1, bf16[4,128,512]{2,1,0:T(8,128)(2,1)S(1)} %get-tuple-element.20.qt_ref, ...), custom_call_target="tpu_custom_call", output_to_operand_aliasing={{0}: (2, {}), {1}: (3, {})} | custom-call | flops 1024 | bytes 1024 | tf_op jit(solution)/shard_map/pallas_call | solution.py:158
Async XLA Ops:
  0.6 2.4 %copy-start = (bf16[512,512]{1,0:T(8,128)(2,1)S(1)}, bf16[512,512]{1,0:T(8,128)(2,1)}, u32[]{:S(2)}) copy-start(bf16[512,512]{1,0:T(8,128)(2,1)} %q_ref.1) | copy-start | bytes 1572868
  0.6 2.4 %copy-start.1 = (s32[16]{0:T(128)S(1)}, s32[16]{0:T(128)}, u32[]{:S(2)}) copy-start(s32[16]{0:T(128)} %lengths_ref.7) | copy-start | bytes 196
  1.7 9.9 %collective-permute-start = (bf16[2,512,128]{2,1,0:T(8,128)(2,1)S(1)}, bf16[2,512,128]{2,1,0:T(8,128)(2,1)S(1)}, u32[]{:S(2)}, u32[]{:S(2)}) collective-permute-start(bf16[2,512,128]{2,1,0:T(8,128)(2,1)S(1)} %pad_maximum_fusion.kv_ref), channel_id=1, source_target_pairs={{0,2},{1,3},{2,4},{3,5},{4,6},{5,7},{8,10},{9,11},{10,12},{11,13},... | collective-permute-start | bytes 786440 | tf_op jit(solution)/shard_map/ppermute | solution.py:176
  5.4 12.3 %collective-permute-start.2 = (bf16[2,512,128]{2,1,0:T(8,128)(2,1)S(1)}, bf16[2,512,128]{2,1,0:T(8,128)(2,1)S(1)}, u32[]{:S(2)}, u32[]{:S(2)}) collective-permute-start(bf16[2,512,128]{2,1,0:T(8,128)(2,1)S(1)} %pad_maximum_fusion.kv_ref), channel_id=1, source_target_pairs={{0,1},{2,3},{4,5},{6,7},{8,9},{10,11},{12,13},{14,15},{16,17},{18,... | collective-permute-start | bytes 786440 | tf_op jit(solution)/shard_map/ppermute | solution.py:176
  8.8 12.6 %collective-permute-start.3 = (bf16[2,512,128]{2,1,0:T(8,128)(2,1)S(1)}, bf16[2,512,128]{2,1,0:T(8,128)(2,1)S(1)}, u32[]{:S(2)}, u32[]{:S(2)}) collective-permute-start(bf16[2,512,128]{2,1,0:T(8,128)(2,1)S(1)} %pad_maximum_fusion.kv_ref), channel_id=1, source_target_pairs={{1,6},{9,14},{17,22},{25,30}} | collective-permute-start | bytes 786440 | tf_op jit(solution)/shard_map/ppermute | solution.py:176
  11.6 13.9 %collective-permute-start.1 = (bf16[2,512,128]{2,1,0:T(8,128)(2,1)S(1)}, bf16[2,512,128]{2,1,0:T(8,128)(2,1)S(1)}, u32[]{:S(2)}, u32[]{:S(2)}) collective-permute-start(bf16[2,512,128]{2,1,0:T(8,128)(2,1)S(1)} %collective-permute-done.refs_0_), channel_id=1, source_target_pairs={{2,4},{3,5},{4,6},{5,7},{10,12},{11,13},{12,14},{13,15},{18,20},{1... | collective-permute-start | bytes 786440 | tf_op jit(solution)/shard_map/ppermute | solution.py:176
  12.9 19.6 %collective-permute-start.4 = (bf16[2,512,128]{2,1,0:T(8,128)(2,1)S(1)}, bf16[2,512,128]{2,1,0:T(8,128)(2,1)S(1)}, u32[]{:S(2)}, u32[]{:S(2)}) collective-permute-start(bf16[2,512,128]{2,1,0:T(8,128)(2,1)S(1)} %collective-permute-done.refs_0_), channel_id=1, source_target_pairs={{3,2},{5,4},{7,6},{2,3},{4,5},{6,7},{11,10},{13,12},{15,14},{10,11... | collective-permute-start | bytes 786440 | tf_op jit(solution)/shard_map/ppermute | solution.py:176
  16.4 21.1 %collective-permute-start.5 = (bf16[2,512,128]{2,1,0:T(8,128)(2,1)S(1)}, bf16[2,512,128]{2,1,0:T(8,128)(2,1)S(1)}, u32[]{:S(2)}, u32[]{:S(2)}) collective-permute-start(bf16[2,512,128]{2,1,0:T(8,128)(2,1)S(1)} %collective-permute-done.refs_0_), channel_id=1, source_target_pairs={{3,4},{5,6},{2,5},{4,7},{11,12},{13,14},{10,13},{12,15},{19,20},{2... | collective-permute-start | bytes 786440 | tf_op jit(solution)/shard_map/ppermute | solution.py:176

commit v2 on v1

--- a/solution.py
+++ b/solution.py
@@ -30,7 +30,7 @@
     for d in range(lengths_ref.shape[0]):
         end = end + lengths_ref[d]
         ends.append(end - own_first)
-    values_t = jnp.transpose(kv_ref[1])
+    values_t = jnp.transpose(kv_ref[q_rows:])
     for h in range(QH):
         qt_ref[h] = jnp.transpose(q_ref[:, h * HD : (h + 1) * HD])
     for t in range(q_rows // tile):
@@ -44,7 +44,7 @@
         hidden = (key < start) | (key > row)
         hidden = jnp.concatenate([hidden] * QH, axis=1)
         heads = jnp.concatenate([qt_ref[h, :, here] for h in range(QH)], axis=1)
-        scores = jnp.where(hidden, LOW, dot(kv_ref[0, :keys, :], heads))
+        scores = jnp.where(hidden, LOW, dot(kv_ref[:keys, :], heads))
         top = jnp.max(scores, axis=0, keepdims=True)
         weights = jnp.exp2((scores - top) * EXP2_SCALE)
         total = jnp.sum(weights, axis=0, keepdims=True)
@@ -82,7 +82,7 @@
         cols = slice(t * tile, (t + 1) * tile)
         live = lax.broadcasted_iota(jnp.int32, (1, tile), 1) + t * tile < live_rows
         live = side_by_side(lambda h: live)
-        scores = dot(kv_ref[0, skipped:], side_by_side(lambda h: qt_ref[h, :, cols]))
+        scores = dot(kv_ref[skipped:q_rows], side_by_side(lambda h: qt_ref[h, :, cols]))
         if cut is not None:
             hidden = lax.broadcasted_iota(jnp.int32, scores.shape, 0) + skipped < cut
             scores = jnp.where(hidden, LOW, scores)
@@ -92,7 +92,7 @@
         top = jnp.where(live, top, old_top)
         weights = jnp.exp2((scores - top) * EXP2_SCALE)
         total = jnp.sum(weights, axis=0, keepdims=True)
-        mixed = dot(jnp.transpose(kv_ref[1, skipped:]), weights.astype(jnp.bfloat16))
+        mixed = dot(jnp.transpose(kv_ref[q_rows + skipped :]), weights.astype(jnp.bfloat16))
         decay = jnp.exp2((old_top - top) * EXP2_SCALE)
         total = old_total * decay + jnp.where(live, total, 0.0)
         mixed = jnp.where(live, mixed, 0.0)
@@ -175,35 +175,36 @@
     def send(value, pairs):
         return lax.ppermute(value, "ctx", pairs)
 
-    own = jnp.stack([key_rows, values])
+    own = jnp.concatenate([key_rows, values])
     moving = send(own, [(i, i + 2) for i in range(count - 2)])
     qt, state = own_part(lengths, queries, own)
     own, *state = lax.optimization_barrier((own, *state))
-    beside = send(own, [(i, i + 1) for i in range(0, count, 2)])
+    pairs = [(i, i + 1) for i in range(0, count, 2)]
+    if reach % 2 == 1:
+        pairs += [(i + 1, i) for i in range(0, count - reach - 1, 2)]
+    beside = first_beside = send(own, pairs)
+    moving, *state = lax.optimization_barrier((moving, *state))
     side = [((0, 1), beside)]
-    if reach % 2 == 1:
-        far = send(own, [(i, i + reach) for i in range(1, count - reach, 2)])
-        side.append(((reach, 0), far))
-    moving, *state = lax.optimization_barrier((moving, *state))
     for k in range(1, strides + 1):
         arrived = moving
-        shards = [((2 * k, 2 * k), arrived)] + side
         if k < strides:
             moving = send(arrived, [(i, i + 2) for i in range(2 * k, count - 2)])
-            exchange = [(i + 1, i) for i in range(2 * k, count, 2)]
+        exchange = [(i + 1, i) for i in range(2 * k, count, 2)]
+        distances = (2 * k - 1, 0)
+        if 2 * k + 1 <= reach:
             exchange += [(i, i + 1) for i in range(2 * k, count, 2)]
-            side = [((2 * k - 1, 2 * k + 1), send(arrived, exchange))]
-        if k == strides - 1:
-            across = [(i, i + 1) for i in range(2 * k + 1, count - 1, 2)]
-            across_distances = (2 * k + 1, 0)
-            if 2 * k + 3 <= reach:
-                across += [(i, i + 3) for i in range(2 * k, count - 3, 2)]
-                across_distances = (2 * k + 1, 2 * k + 3)
-            late = [(across_distances, send(arrived, across))]
+            distances = (2 * k - 1, 2 * k + 1)
+        shards = [((2 * k, 2 * k), arrived)] + side
+        side = [(distances, send(arrived, exchange))]
         state = past_part(lengths, qt, state, shards)
+        if k == strides - 1 and reach % 2 == 1:
+            first_beside, *state = lax.optimization_barrier((first_beside, *state))
+            far = send(first_beside, [(i, i + reach + 1) for i in range(0, count - reach - 1, 2)])
         if k < strides:
             moving, *state = lax.optimization_barrier((moving, *state))
-    return past_part(lengths, qt, state, late, is_last=True)
+    if reach % 2 == 1:
+        side.insert(0, ((reach, 0), far))
+    return past_part(lengths, qt, state, side, is_last=True)
 
 
 def solution(mesh):

time: 40.4 us -> 36.3 us (0.90)
  the two profiles are of different devices: /device:TPU:24 before, /device:TPU:18 now
where the time goes in v2:
time: 36.3 us; the launch traced here: 36 us
  starting transfers between devices  19.2 us (53%)
  Pallas kernels  13.1 us (36%)
  local copies, waits for them, and re-layouts  2.02 us (6%)
  waiting for transfers between devices  0.92 us (3%)
  between operations  0.79 us (2%)
    ppermute x6, starting transfers between devices, send(): return lax.ppermute(value, 'ctx', pairs)  19.2 us
    pallas_call x3, Pallas kernels, past_part(): pl.pallas_call(functools.partial(past_kernel, distances, is_last), out_sh...  10.7 us
    pallas_call x1, Pallas kernels, own_part(): pl.pallas_call(own_kernel, out_shape=(jax.ShapeDtypeStruct((QH, HD, q_row...  2.34 us
    unnamed x7, local copies, waits for them, and re-layouts  2 us
    ppermute x6, waiting for transfers between devices, send(): return lax.ppermute(value, 'ctx', pairs)  0.92 us
  transfers between devices with their start and end apart: 6, of which 1 were waited for; matrix products, arithmetic and copies ran while one was open for 0% of the time, Pallas kernels for 25%

profile of v2, /device:TPU:18, one launch (start us, length us, event | category | flops | bytes accessed | tf_op | source)
XLA Modules:
  0.0 36.0 jit_solution(17941642897849773342)
XLA Ops:
  0.6 0.0 copy-start.2
  0.6 0.9 %constant_dynamic-update-slice_fusion.1 = bf16[1024,128]{1,0:T(8,128)(2,1)S(1)} fusion(bf16[512,128]{1,0:T(8,128)(2,1)} %param.6), kind=kLoop, calls=%fused_computation.1 | loop fusion | bytes 262144
  1.6 0.0 copy-done.2
  1.6 0.0 copy-start.1
  1.6 3.5 %collective-permute-start = (bf16[1024,128]{1,0:T(8,128)(2,1)S(1)}, bf16[1024,128]{1,0:T(8,128)(2,1)S(1)}, u32[]{:S(2)}, u32[]{:S(2)}) collective-permute-start(bf16[1024,128]{1,0:T(8,128)(2,1)S(1)} %constant_dynamic-update-slice_fusion.kv_ref), channel_id=1, source_target_pairs={{0,2},{1,3},{2,4},{3,5},{4,6},{5,7},{8,10},{9,11},{10,12},{11,13},... | collective-permute-start | bytes 786440 | tf_op jit(solution)/shard_map/ppermute | solution.py:176
  5.1 0.0 copy-done.1
  5.1 0.0 copy-start
  5.2 1.0 %copy-done = bf16[512,512]{1,0:T(8,128)(2,1)S(1)} copy-done((bf16[512,512]{1,0:T(8,128)(2,1)S(1)}, bf16[512,512]{1,0:T(8,128)(2,1)}, u32[]{:S(2)}) %copy-start) | copy-done | bytes 524312
  6.2 2.3 %shard_map.59 = (bf16[4,128,512]{2,1,0:T(8,128)(2,1)S(1)}, f32[4,128,512]{2,1,0:T(8,128)S(1)}, f32[8,512]{1,0:T(8,128)S(1)}) custom-call(s32[16]{0:T(128)S(1)} %copy-done.1, bf16[512,512]{1,0:T(8,128)(2,1)S(1)} %copy-done, bf16[1024,128]{1,0:T(8,128)(2,1)S(1)} %constant_dynamic-update-slice_fusion.kv_ref), custom_call_target="tpu_custom_call" | custom-call | flops 1024 | bytes 1024 | tf_op jit(solution)/shard_map/pallas_call | solution.py:135
  8.5 3.4 %collective-permute-start.2 = (bf16[1024,128]{1,0:T(8,128)(2,1)S(1)}, bf16[1024,128]{1,0:T(8,128)(2,1)S(1)}, u32[]{:S(2)}, u32[]{:S(2)}) collective-permute-start(bf16[1024,128]{1,0:T(8,128)(2,1)S(1)} %constant_dynamic-update-slice_fusion.kv_ref), channel_id=1, source_target_pairs={{0,1},{2,3},{4,5},{6,7},{1,0},{8,9},{10,11},{12,13},{14,15},{9,8},... | collective-permute-start | bytes 786440 | tf_op jit(solution)/shard_map/ppermute | solution.py:176
  12.0 0.0 collective-permute-done.refs_0_
  12.0 3.1 %collective-permute-start.1 = (bf16[1024,128]{1,0:T(8,128)(2,1)S(1)}, bf16[1024,128]{1,0:T(8,128)(2,1)S(1)}, u32[]{:S(2)}, u32[]{:S(2)}) collective-permute-start(bf16[1024,128]{1,0:T(8,128)(2,1)S(1)} %collective-permute-done.refs_0_), channel_id=1, source_target_pairs={{2,4},{3,5},{4,6},{5,7},{10,12},{11,13},{12,14},{13,15},{18,20},{1... | collective-permute-start | bytes 786440 | tf_op jit(solution)/shard_map/ppermute | solution.py:176
  15.1 3.4 %collective-permute-start.3 = (bf16[1024,128]{1,0:T(8,128)(2,1)S(1)}, bf16[1024,128]{1,0:T(8,128)(2,1)S(1)}, u32[]{:S(2)}, u32[]{:S(2)}) collective-permute-start(bf16[1024,128]{1,0:T(8,128)(2,1)S(1)} %collective-permute-done.refs_0_), channel_id=1, source_target_pairs={{3,2},{5,4},{7,6},{2,3},{4,5},{6,7},{11,10},{13,12},{15,14},{10,11... | collective-permute-start | bytes 786440 | tf_op jit(solution)/shard_map/ppermute | solution.py:176
  18.5 0.0 collective-permute-done.2.refs_1_
  18.5 2.7 %shard_map.60 = (f32[4,128,512]{2,1,0:T(8,128)S(1)}, f32[8,512]{1,0:T(8,128)S(1)}) custom-call(s32[16]{0:T(128)S(1)} %copy-done.1, bf16[4,128,512]{2,1,0:T(8,128)(2,1)S(1)} %get-tuple-element.23.qt_ref, f32[4,128,512]{2,1,0:T(8,128)S(1)} %get-tuple-element.30.acc_in, ...), custom_call_target="tpu_custom_call", output_to_operand_aliasing={{0}: (2, {}), {1}: (3, {})} | custom-call | flops 1024 | bytes 1024 | tf_op jit(solution)/shard_map/pallas_call | solution.py:158
  21.2 0.7 %collective-permute-start.4 = (bf16[1024,128]{1,0:T(8,128)(2,1)S(1)}, bf16[1024,128]{1,0:T(8,128)(2,1)S(1)}, u32[]{:S(2)}, u32[]{:S(2)}) collective-permute-start(bf16[1024,128]{1,0:T(8,128)(2,1)S(1)} %collective-permute-done.2.refs_1_), channel_id=1, source_target_pairs={{0,6},{8,14},{16,22},{24,30}} | collective-permute-start | bytes 786440 | tf_op jit(solution)/shard_map/ppermute | solution.py:176
  21.9 0.0 collective-permute-done.1.refs_0_
  21.9 5.1 %collective-permute-start.5 = (bf16[1024,128]{1,0:T(8,128)(2,1)S(1)}, bf16[1024,128]{1,0:T(8,128)(2,1)S(1)}, u32[]{:S(2)}, u32[]{:S(2)}) collective-permute-start(bf16[1024,128]{1,0:T(8,128)(2,1)S(1)} %collective-permute-done.1.refs_0_), channel_id=1, source_target_pairs={{5,4},{7,6},{4,5},{6,7},{13,12},{15,14},{12,13},{14,15},{21,20},{2... | collective-permute-start | bytes 786440 | tf_op jit(solution)/shard_map/ppermute | solution.py:176
  27.0 0.0 collective-permute-done.3.refs_1_
  27.1 4.1 %shard_map.61 = (f32[4,128,512]{2,1,0:T(8,128)S(1)}, f32[8,512]{1,0:T(8,128)S(1)}) custom-call(s32[16]{0:T(128)S(1)} %copy-done.1, bf16[4,128,512]{2,1,0:T(8,128)(2,1)S(1)} %get-tuple-element.23.qt_ref, f32[4,128,512]{2,1,0:T(8,128)S(1)} %get-tuple-element.36.acc_in, ...), custom_call_target="tpu_custom_call", output_to_operand_aliasing={{0}: (2, {}), {1}: (3, {})} | custom-call | flops 1024 | bytes 1024 | tf_op jit(solution)/shard_map/pallas_call | solution.py:158
  31.2 0.0 collective-permute-done.4.refs_0_
  31.2 0.9 %collective-permute-done.5.refs_1_ = bf16[1024,128]{1,0:T(8,128)(2,1)S(1)} collective-permute-done((bf16[1024,128]{1,0:T(8,128)(2,1)S(1)}, bf16[1024,128]{1,0:T(8,128)(2,1)S(1)}, u32[]{:S(2)}, u32[]{:S(2)}) %collective-permute-start.5) | collective-permute-done | bytes 262176 | tf_op jit(solution)/shard_map/ppermute | solution.py:176
  32.1 3.9 %shard_map.62 = (f32[4,128,512]{2,1,0:T(8,128)S(1)}, f32[8,512]{1,0:T(8,128)S(1)}, bf16[512,512]{1,0:T(8,128)(2,1)}, f32[4,512]{1,0:T(4,128)}) custom-call(s32[16]{0:T(128)S(1)} %copy-done.1, bf16[4,128,512]{2,1,0:T(8,128)(2,1)S(1)} %get-tuple-element.23.qt_ref, ...), custom_call_target="tpu_custom_call", output_to_operand_aliasing={{0}: (2, {}), {1}: (3, {})} | custom-call | flops 1024 | bytes 1024 | tf_op jit(solution)/shard_map/pallas_call | solution.py:158
  (1 shorter events, 0.0 us)
Async XLA Ops:
  0.6 1.0 %copy-start.2 = (bf16[512,128]{1,0:T(8,128)(2,1)S(1)}, bf16[512,128]{1,0:T(8,128)(2,1)}, u32[]{:S(2)}) copy-start(bf16[512,128]{1,0:T(8,128)(2,1)} %param.7) | copy-start | bytes 393220
  1.6 3.5 %copy-start.1 = (s32[16]{0:T(128)S(1)}, s32[16]{0:T(128)}, u32[]{:S(2)}) copy-start(s32[16]{0:T(128)} %lengths_ref.7) | copy-start | bytes 196
  1.6 10.3 %collective-permute-start = (bf16[1024,128]{1,0:T(8,128)(2,1)S(1)}, bf16[1024,128]{1,0:T(8,128)(2,1)S(1)}, u32[]{:S(2)}, u32[]{:S(2)}) collective-permute-start(bf16[1024,128]{1,0:T(8,128)(2,1)S(1)} %constant_dynamic-update-slice_fusion.kv_ref), channel_id=1, source_target_pairs={{0,2},{1,3},{2,4},{3,5},{4,6},{5,7},{8,10},{9,11},{10,12},{11,13},... | collective-permute-start | bytes 786440 | tf_op jit(solution)/shard_map/ppermute | solution.py:176
  5.1 1.0 %copy-start = (bf16[512,512]{1,0:T(8,128)(2,1)S(1)}, bf16[512,512]{1,0:T(8,128)(2,1)}, u32[]{:S(2)}) copy-start(bf16[512,512]{1,0:T(8,128)(2,1)} %q_ref.1) | copy-start | bytes 1572868
  8.5 10.0 %collective-permute-start.2 = (bf16[1024,128]{1,0:T(8,128)(2,1)S(1)}, bf16[1024,128]{1,0:T(8,128)(2,1)S(1)}, u32[]{:S(2)}, u32[]{:S(2)}) collective-permute-start(bf16[1024,128]{1,0:T(8,128)(2,1)S(1)} %constant_dynamic-update-slice_fusion.kv_ref), channel_id=1, source_target_pairs={{0,1},{2,3},{4,5},{6,7},{1,0},{8,9},{10,11},{12,13},{14,15},{9,8},... | collective-permute-start | bytes 786440 | tf_op jit(solution)/shard_map/ppermute | solution.py:176
  12.0 9.9 %collective-permute-start.1 = (bf16[1024,128]{1,0:T(8,128)(2,1)S(1)}, bf16[1024,128]{1,0:T(8,128)(2,1)S(1)}, u32[]{:S(2)}, u32[]{:S(2)}) collective-permute-start(bf16[1024,128]{1,0:T(8,128)(2,1)S(1)} %collective-permute-done.refs_0_), channel_id=1, source_target_pairs={{2,4},{3,5},{4,6},{5,7},{10,12},{11,13},{12,14},{13,15},{18,20},{1... | collective-permute-start | bytes 786440 | tf_op jit(solution)/shard_map/ppermute | solution.py:176
  15.1 12.0 %collective-permute-start.3 = (bf16[1024,128]{1,0:T(8,128)(2,1)S(1)}, bf16[1024,128]{1,0:T(8,128)(2,1)S(1)}, u32[]{:S(2)}, u32[]{:S(2)}) collective-permute-start(bf16[1024,128]{1,0:T(8,128)(2,1)S(1)} %collective-permute-done.refs_0_), channel_id=1, source_target_pairs={{3,2},{5,4},{7,6},{2,3},{4,5},{6,7},{11,10},{13,12},{15,14},{10,11... | collective-permute-start | bytes 786440 | tf_op jit(solution)/shard_map/ppermute | solution.py:176
  21.2 10.0 %collective-permute-start.4 = (bf16[1024,128]{1,0:T(8,128)(2,1)S(1)}, bf16[1024,128]{1,0:T(8,128)(2,1)S(1)}, u32[]{:S(2)}, u32[]{:S(2)}) collective-permute-start(bf16[1024,128]{1,0:T(8,128)(2,1)S(1)} %collective-permute-done.2.refs_1_), channel_id=1, source_target_pairs={{0,6},{8,14},{16,22},{24,30}} | collective-permute-start | bytes 786440 | tf_op jit(solution)/shard_map/ppermute | solution.py:176
  21.9 10.2 %collective-permute-start.5 = (bf16[1024,128]{1,0:T(8,128)(2,1)S(1)}, bf16[1024,128]{1,0:T(8,128)(2,1)S(1)}, u32[]{:S(2)}, u32[]{:S(2)}) collective-permute-start(bf16[1024,128]{1,0:T(8,128)(2,1)S(1)} %collective-permute-done.1.refs_0_), channel_id=1, source_target_pairs={{5,4},{7,6},{4,5},{6,7},{13,12},{15,14},{12,13},{14,15},{21,20},{2... | collective-permute-start | bytes 786440 | tf_op jit(solution)/shard_map/ppermute | solution.py:176
